TPU v7x, 256 devices: a whole 4x4x8 slice. The times are simulated.
256 devices in a mesh: dom: 64 (over z, y, core), rep: 4 (over x).
Axes of the slice: x: 4, y: 4, z: 8, core: 2. Of those that a mesh axis runs over, the one named last changes fastest.
Arguments:
- features: bfloat16 [65536, 512], P('dom', 'rep'), may hold values from -6 to 6
- weight: bfloat16 [512, 512], P(None, 'rep'), may hold values from -0.25 to 0.25
- bias: bfloat16 [512], P('rep'), may hold values from -3 to 3
- cotangent: bfloat16 [65536, 512], P('dom', 'rep'), may hold values from -6 to 6
- tile_vals: bfloat16 [64, 160, 128, 128], P('dom'), may hold values from -0.21875 to 0.21875
- tile_row: int32 [64, 160], P('dom'), may hold values from 0 to 8, as said below
- tile_src: int32 [64, 160], P('dom'), may hold values from 0 to 135, as said below
- send_blocks: int32 [64, 64, 2], P('dom'), may hold values from 0 to 7
- send_count: int32 [64, 64], P('dom'), may hold values from 0 to 2, as said below
Outputs:
- out: bfloat16 [65536, 512], P('dom', 'rep')
- grad_input: bfloat16 [65536, 512], P('dom', 'rep')
- grad_weight: float32 [512, 512], P(None, 'rep')
- grad_bias: float32 [512], P('rep')
Inputs may be any that keep to these rules, and one draw needn't show every extreme that they name: Partition q sends the first send_count[q, p] entries of send_blocks[q, p] to partition p; send_count[q, q] = 0, and every partition sends 2 blocks to some partition. `tile_row`: 8 marks an unused slot. Slots below 32 take own blocks; slot 32 + q * 2 + c is used only if c < send_count[q, p]. Partition 0 uses all its own-block slots. `tile_src`: slots below 32 name an own block below 8; slot 32 + m names source slot 8 + m.
All inputs are finite; a program needn't handle non-finite values.
Results may differ from a plain program's by a relative error of at most 0.007.
Values may be sent and summed in bfloat16 or wider, within the bound.
A program may use at most 128 MiB of HBM per device.

v0:
```python
import jax
import jax.numpy as jnp
from jax import lax
from jax.sharding import PartitionSpec as P

B = 128
NB = 8
CAP = 2


def receive_blocks(outgoing, peer_count, panel_width):
    arrived = lax.all_to_all(outgoing, "dom", split_axis=0, concat_axis=0, tiled=True)
    return arrived.reshape(peer_count * CAP, B, panel_width)


def shards(
    features, weight, bias, cotangent, tile_vals, tile_row, tile_src, send_blocks, send_count
):
    row_count, panel_width = features.shape
    peer_count = lax.axis_size("dom")
    gathered = lax.all_gather(features, "rep", axis=1, tiled=True)
    hidden = jnp.dot(gathered, weight, preferred_element_type=jnp.float32).astype(jnp.bfloat16)
    hidden_blocks = hidden.reshape(NB, B, panel_width)
    targets = send_blocks[0]
    counts = send_count[0]
    keep_slot = jnp.arange(CAP, dtype=jnp.int32)[None, :] < counts[:, None]
    outgoing = hidden_blocks[targets]
    outgoing = jnp.where(keep_slot[:, :, None, None], outgoing, jnp.zeros_like(outgoing))
    tile_set = tile_vals[0]
    tile_rows = tile_row[0]
    tile_sources = tile_src[0]
    arrived = receive_blocks(outgoing, peer_count, panel_width)
    sources = jnp.concatenate([hidden_blocks, arrived], 0)
    product = jnp.einsum(
        "kab,kbf->kaf", tile_set, sources[tile_sources], preferred_element_type=jnp.float32
    )
    aggregate = jax.ops.segment_sum(product, tile_rows, NB + 1)[:NB]
    shifted = aggregate.reshape(row_count, panel_width) + bias.astype(jnp.float32)
    sigma = jax.nn.sigmoid(shifted)
    out = (shifted * sigma).astype(jnp.bfloat16)
    grad_pre = (cotangent.astype(jnp.float32) * sigma * (1.0 + shifted * (1.0 - sigma))).astype(
        jnp.bfloat16
    )
    pre_padded = jnp.concatenate(
        [grad_pre.reshape(NB, B, panel_width), jnp.zeros((1, B, panel_width), jnp.bfloat16)], 0
    )
    contrib = jnp.einsum(
        "kab,kaf->kbf", tile_set, pre_padded[tile_rows], preferred_element_type=jnp.float32
    )
    per_slot = jax.ops.segment_sum(contrib, tile_sources, NB + peer_count * CAP)
    outbound = per_slot[NB:].reshape(peer_count, CAP, B, panel_width)
    returned = lax.all_to_all(outbound, "dom", split_axis=0, concat_axis=0, tiled=True)
    own_blocks = per_slot[:NB]
    returned = jnp.where(keep_slot[:, :, None, None], returned, jnp.zeros_like(returned))
    grad_blocks = own_blocks + jax.ops.segment_sum(
        returned.reshape(peer_count * CAP, B, panel_width), targets.reshape(-1), NB
    )
    grad_agg = grad_blocks.reshape(row_count, panel_width).astype(jnp.bfloat16)
    weight_part = jnp.dot(gathered.T, grad_agg, preferred_element_type=jnp.float32)
    bias_part = jnp.sum(grad_pre.astype(jnp.float32), 0)
    grad_weight, grad_bias = lax.psum((weight_part, bias_part), "dom")
    partial_terms = jnp.dot(grad_agg, weight.T, preferred_element_type=jnp.float32)
    grad_input = lax.psum_scatter(partial_terms, "rep", scatter_dimension=1, tiled=True).astype(
        jnp.bfloat16
    )
    return (out, grad_input, grad_weight, grad_bias)


def solution(mesh):
    in_specs = (
        P("dom", "rep"),
        P(None, "rep"),
        P("rep"),
        P("dom", "rep"),
        P("dom", None, None, None),
        P("dom", None),
        P("dom", None),
        P("dom", None, None),
        P("dom", None),
    )
    out_specs = (P("dom", "rep"), P("dom", "rep"), P(None, "rep"), P("rep"))
    return jax.shard_map(shards, mesh=mesh, in_specs=in_specs, out_specs=out_specs, check_vma=False)
```

profile of v0, /device:TPU:1, one launch (start us, length us, event | category | flops | bytes accessed | tf_op | source)
XLA Modules:
  0.0 723.8 jit_solution(12466726873163206390)
XLA Ops:
  7.9 0.7 compare_select_fusion.2
  8.9 0.7 iota_compare_fusion
  9.6 31.6 %all-gather.2.cloned.1.call-done = bf16[1024,512]{1,0:T(8,128)(2,1)} async-done(((bf16[1024,128]{1,0:T(8,128)(2,1)}), bf16[1024,512]{1,0:T(8,128)(2,1)}) %all-gather.2.cloned.1.call-update) | async-done | bytes 1048592 | tf_op jit(solution)/shard_map/all_gather | solution.py:21
  41.2 1.7 convolution_convert_fusion
  42.8 3.0 gather_fusion
  45.9 4.5 broadcast_select_fusion.1
  50.4 11.9 %all-to-all-start = ((bf16[64,2,128,128]{3,2,1,0:T(8,128)(2,1)}), bf16[64,2,128,128]{3,2,1,0:T(8,128)(2,1)}, u32[]{:S(2)}, u32[]{:S(2)}) async-start(bf16[64,2,128,128]{3,2,1,0:T(8,128)(2,1)} %broadcast_select_fusion.1), calls=%async_computation | async-start | bytes 8388608 | tf_op jit(solution)/shard_map/all_to_all | solution.py:12
  62.4 94.3 %all-to-all-done = bf16[64,2,128,128]{3,2,1,0:T(8,128)(2,1)} async-done(((bf16[64,2,128,128]{3,2,1,0:T(8,128)(2,1)}), bf16[64,2,128,128]{3,2,1,0:T(8,128)(2,1)}, u32[]{:S(2)}, u32[]{:S(2)}) %all-to-all-start) | async-done | bytes 4194336 | tf_op jit(solution)/shard_map/all_to_all | solution.py:12
  156.7 4.6 pad_maximum_fusion
  161.3 10.0 %gather_fusion.1 = bf16[160,128,128]{2,1,0:T(8,128)(2,1)} fusion(bf16[136,128,128]{2,1,0:T(8,128)(2,1)} %pad_maximum_fusion, s32[1024]{0:T(1024)S(1)} %pad_clamp_fusion.1), kind=kCustom, calls=%fused_computation.1 | custom fusion | bytes 10486400 | tf_op jit(solution)/shard_map/gather | solution.py:35
  171.3 11.8 %fusion.4 = f32[160,128,128]{1,2,0:T(8,128)} fusion(bf16[160,128,128]{2,1,0:T(8,128)(2,1)} %gather_fusion.1, bf16[1,160,128,128]{3,2,1,0:T(8,128)(2,1)} %param.13), kind=kOutput, calls=%fused_computation.13 | convolution fusion | flops 671088640 | bytes 20971520 | tf_op jit(solution)/shard_map/kab,kbf->kaf/dot_general | solution.py:34
  183.2 11.7 %copy.20 = f32[160,128,128]{2,1,0:T(8,128)} copy(f32[160,128,128]{1,2,0:T(8,128)} %fusion.4) | data formatting | bytes 20971520 | tf_op jit(solution)/shard_map/kab,kbf->kaf/dot_general | solution.py:34
  194.9 21.1 %scatter_fusion = f32[9,128,128]{2,1,0:T(8,128)S(1)} fusion(f32[9,128,128]{2,1,0:T(8,128)S(1)} %broadcast_in_dim.19, s32[160]{0:T(256)S(1)} %bitcast.58, f32[160,128,128]{2,1,0:T(8,128)} %copy.20), kind=kCustom, calls=%fused_computation.3 | custom fusion | flops 2621440 | bytes 31457920 | tf_op jit(solution)/shard_map/scatter-add | solution.py:37
  216.2 1.0 convert_reduce_fusion
  217.2 7.5 %gather_fusion.2 = bf16[160,128,128]{2,1,0:T(8,128)(2,1)} fusion(bf16[9,128,128]{2,1,0:T(8,128)(2,1)S(1)} %concatenate.7, s32[1024]{0:T(1024)S(1)} %pad_clamp_fusion), kind=kCustom, calls=%fused_computation.2 | custom fusion | bytes 10486400 | tf_op jit(solution)/shard_map/gather | solution.py:48
  224.6 9.8 %fusion.7 = f32[160,128,128]{1,2,0:T(8,128)} fusion(bf16[160,128,128]{2,1,0:T(8,128)(2,1)} %gather_fusion.2, bf16[1,160,128,128]{3,2,1,0:T(8,128)(2,1)} %param.13), kind=kOutput, calls=%fused_computation.14 | convolution fusion | flops 671088640 | bytes 20971520 | tf_op jit(solution)/shard_map/kab,kaf->kbf/dot_general | solution.py:47
  234.4 11.8 %copy.22 = f32[160,128,128]{2,1,0:T(8,128)} copy(f32[160,128,128]{1,2,0:T(8,128)} %fusion.7) | data formatting | bytes 20971520 | tf_op jit(solution)/shard_map/kab,kaf->kbf/dot_general | solution.py:47
  246.2 4.6 broadcast_in_dim.38
  250.8 33.2 %scatter_fusion.1 = f32[136,128,128]{2,1,0:T(8,128)} fusion(f32[136,128,128]{2,1,0:T(8,128)} %broadcast_in_dim.38, s32[160]{0:T(256)S(1)} %bitcast.59, f32[160,128,128]{2,1,0:T(8,128)} %copy.22), kind=kCustom, calls=%fused_computation.4 | custom fusion | flops 2621440 | bytes 31457920 | tf_op jit(solution)/shard_map/scatter-add | solution.py:50
  284.0 7.9 %slice.20 = f32[128,128,128]{2,1,0:T(8,128)} slice(f32[136,128,128]{2,1,0:T(8,128)} %scatter_fusion.1), slice={[8:136], [0:128], [0:128]} | slice | bytes 16777216 | tf_op jit(solution)/shard_map/slice | solution.py:51
  291.8 7.6 %all-to-all-start.1 = ((f32[64,2,128,128]{3,2,1,0:T(8,128)}), f32[64,2,128,128]{3,2,1,0:T(8,128)}, u32[]{:S(2)}, u32[]{:S(2)}) async-start(f32[64,2,128,128]{3,2,1,0:T(8,128)} %bitcast.52), calls=%async_computation.1 | async-start | bytes 16777216 | tf_op jit(solution)/shard_map/all_to_all | solution.py:52
  299.7 1.1 slice.19
  300.8 181.5 %all-to-all-done.1 = f32[64,2,128,128]{3,2,1,0:T(8,128)} async-done(((f32[64,2,128,128]{3,2,1,0:T(8,128)}), f32[64,2,128,128]{3,2,1,0:T(8,128)}, u32[]{:S(2)}, u32[]{:S(2)}) %all-to-all-start.1) | async-done | bytes 8388640 | tf_op jit(solution)/shard_map/all_to_all | solution.py:52
  482.3 7.2 broadcast_select_fusion
  489.6 17.0 %scatter_fusion.2 = f32[8,128,128]{2,1,0:T(8,128)S(1)} fusion(f32[8,128,128]{2,1,0:T(8,128)S(1)} %slice.19, s32[128]{0:T(128)S(1)} %reshape.185, f32[128,128,128]{2,1,0:T(8,128)} %bitcast.53), kind=kCustom, calls=%fused_computation.5 | custom fusion | flops 2097152 | bytes 25166336 | tf_op jit(solution)/shard_map/scatter-add | solution.py:55
  506.6 1.0 convolution_bitcast_fusion
  507.7 1.8 fusion.10
  509.6 127.7 %psum.15 = f32[128]{0:T(128)} all-reduce(f32[128]{0:T(128)S(1)} %get-tuple-element.12), channel_id=1, replica_groups=mesh['dom'=64,'rep'=4] {'dom'}, use_global_device_ids=true, to_apply=%region_6.7 | all-reduce | flops 128 | bytes 1024 | tf_op jit(solution)/shard_map/psum | solution.py:61
  637.3 46.1 %all-reduce.3.cloned.1.call-done = f32[512,128]{0,1:T(8,128)} async-done(((f32[512,128]{0,1:T(8,128)}), f32[512,128]{0,1:T(8,128)}) %all-reduce.3.cloned.1.call-update) | async-done | bytes 262160 | tf_op jit(solution)/shard_map/psum | solution.py:61
  683.4 1.8 copy.24
  685.1 30.4 %reduce-scatter.2.cloned.1.call-done = f32[1024,128]{1,0:T(8,128)} async-done(((f32[1024,512]{1,0:T(8,128)}), f32[1024,128]{1,0:T(8,128)}) %reduce-scatter.2.cloned.1.call-update) | async-done | bytes 524304 | tf_op jit(solution)/shard_map/reduce_scatter | solution.py:63
  715.5 1.8 convert_element_type.34
  (34 shorter events, 1.5 us)
Async XLA Ops:
  7.2 34.0 %copy-start = (bf16[512,128]{1,0:T(8,128)(2,1)S(1)}, bf16[512,128]{1,0:T(8,128)(2,1)}, u32[]{:S(2)}) copy-start(bf16[512,128]{1,0:T(8,128)(2,1)} %param.10) | copy-start | bytes 393220
  7.2 34.0 %all-gather.2.cloned.1.call-start = ((), (), s32[]{:S(2)}) async-start(), calls=%async_computation.3 | async-start | bytes 1310720 | tf_op jit(solution)/shard_map/all_gather | solution.py:21
  50.4 11.9 %copy-start.6 = (bf16[128]{0:T(256)(128)(2,1)S(1)}, bf16[128]{0:T(256)(128)(2,1)}, u32[]{:S(2)}) copy-start(bf16[128]{0:T(256)(128)(2,1)} %param.11) | copy-start | bytes 772
  50.4 11.9 %copy-start.4 = (s32[1,160]{1,0:T(1,128)S(1)}, s32[1,160]{1,0:T(1,128)}, u32[]{:S(2)}) copy-start(s32[1,160]{1,0:T(1,128)} %param.15) | copy-start | bytes 1924
  50.4 12.0 %copy-start.3 = (s32[1,160]{1,0:T(1,128)S(1)}, s32[1,160]{1,0:T(1,128)}, u32[]{:S(2)}) copy-start(s32[1,160]{1,0:T(1,128)} %param.14) | copy-start | bytes 1924
  50.4 106.3 %all-to-all-start = ((bf16[64,2,128,128]{3,2,1,0:T(8,128)(2,1)}), bf16[64,2,128,128]{3,2,1,0:T(8,128)(2,1)}, u32[]{:S(2)}, u32[]{:S(2)}) async-start(bf16[64,2,128,128]{3,2,1,0:T(8,128)(2,1)} %broadcast_select_fusion.1), calls=%async_computation | async-start | bytes 8388608 | tf_op jit(solution)/shard_map/all_to_all | solution.py:12
  194.9 21.2 %copy-start.2 = (bf16[1024,128]{1,0:T(8,128)(2,1)S(1)}, bf16[1024,128]{1,0:T(8,128)(2,1)}, u32[]{:S(2)}) copy-start(bf16[1024,128]{1,0:T(8,128)(2,1)} %param.12) | copy-start | bytes 786436
  291.8 7.7 %copy-start.5 = (s32[1,64,2]{1,2,0:T(2,128)S(1)}, s32[1,64,2]{1,2,0:T(2,128)}, u32[]{:S(2)}) copy-start(s32[1,64,2]{1,2,0:T(2,128)} %param.16) | copy-start | bytes 1540
  291.8 190.5 %all-to-all-start.1 = ((f32[64,2,128,128]{3,2,1,0:T(8,128)}), f32[64,2,128,128]{3,2,1,0:T(8,128)}, u32[]{:S(2)}, u32[]{:S(2)}) async-start(f32[64,2,128,128]{3,2,1,0:T(8,128)} %bitcast.52), calls=%async_computation.1 | async-start | bytes 16777216 | tf_op jit(solution)/shard_map/all_to_all | solution.py:52
  299.4 383.9 %all-reduce.3.cloned.1.call-start = ((), (), s32[]{:S(2)}) async-start(), calls=%async_computation.5 | async-start | bytes 524288 | tf_op jit(solution)/shard_map/psum | solution.py:61
  489.5 17.1 %copy-start.1 = (bf16[1024,512]{1,0:T(8,128)(2,1)S(1)}, bf16[1024,512]{1,0:T(8,128)(2,1)}, u32[]{:S(2)}) copy-start(bf16[1024,512]{1,0:T(8,128)(2,1)} %all-gather.2.cloned.1.call-done) | copy-start | bytes 3145732
  507.7 207.8 %reduce-scatter.2.cloned.1.call-start = ((), (), s32[]{:S(2)}) async-start(), calls=%async_computation.4 | async-start | bytes 2621440 | tf_op jit(solution)/shard_map/reduce_scatter | solution.py:63
Sparse Core Ops, SparseCore 0:
  9.8 31.3 all-gather.1
  507.8 175.4 all-reduce.2
  686.1 29.4 reduce-scatter.1
where the time goes:
time: 726 us; the launch traced here: 724 us
  waiting for transfers between devices  385 us (53%)
  blocking collectives  128 us (18%)
  other arithmetic  91.9 us (13%)
  local copies, waits for them, and re-layouts  60 us (8%)
  matrix products  26.1 us (4%)
  starting transfers between devices  19.6 us (3%)
  between operations  13.9 us (2%)
    all_to_all x1, waiting for transfers between devices, shards(): lax.all_to_all(outbound, 'dom', split_axis=0, concat_axis=0, tiled=True)  182 us
    psum x1, blocking collectives, shards(): grad_weight, grad_bias = lax.psum((weight_part, bias_part), 'dom')  128 us
    all_to_all x1, waiting for transfers between devices, receive_blocks(): lax.all_to_all(outgoing, 'dom', split_axis=0, concat_axis=0, tiled=True)  94.3 us
    psum x1, waiting for transfers between devices, shards(): grad_weight, grad_bias = lax.psum((weight_part, bias_part), 'dom')  46.1 us
    scatter-add x1, other arithmetic, shards(): per_slot = jax.ops.segment_sum(contrib, tile_sources, NB + peer_count * CAP)  33.2 us
    all_gather x1, waiting for transfers between devices, shards(): gathered = lax.all_gather(features, 'rep', axis=1, tiled=True)  31.6 us
    reduce_scatter x1, waiting for transfers between devices, shards(): lax.psum_scatter(partial_terms, 'rep', scatter_dimension=1, tiled=True)  30.4 us
    scatter-add x1, other arithmetic, shards(): aggregate = jax.ops.segment_sum(product, tile_rows, NB + 1)[:NB]  21.1 us
  transfers between devices with their start and end apart: 5, of which 5 were waited for; matrix products, arithmetic and copies ran while one was open for 1% of the time, Pallas kernels for 0%

commit v1 on v0

--- a/solution.py
+++ b/solution.py
@@ -18,7 +18,9 @@
 ):
     row_count, panel_width = features.shape
     peer_count = lax.axis_size("dom")
-    gathered = lax.all_gather(features, "rep", axis=1, tiled=True)
+    gathered = jnp.concatenate(
+        lax.all_to_all(jnp.stack([features] * lax.axis_size("rep")), "rep", 0, 0), axis=1
+    )
     hidden = jnp.dot(gathered, weight, preferred_element_type=jnp.float32).astype(jnp.bfloat16)
     hidden_blocks = hidden.reshape(NB, B, panel_width)
     targets = send_blocks[0]

time: 726 us -> 684 us (0.942)
  waiting for transfers between devices: 385 us -> 332 us
  starting transfers between devices: 19.6 us -> 27.4 us
    all_gather x1 -> x0, waiting for transfers between devices: 31.6 us -> none  [shards(): gathered = lax.all_gather(features, 'rep', axis=1, tiled=True)]
    reduce_scatter x1, waiting for transfers between devices: 30.4 us -> 0.01 us  [shards(): lax.psum_scatter(partial_terms, 'rep', scatter_dimension=1, tiled=True)]
    all_to_all x0 -> x1, waiting for transfers between devices: none -> 11.6 us  [shards(): lax.all_to_all(jnp.stack([features] * lax.axis_size('rep')), 'rep', 0, 0)]
  transfers between devices with their start and end apart: 5 -> 5, of which waited for: 5 -> 4; matrix products, arithmetic and copies ran while one was open for 1% -> 1% of each run, Pallas kernels for 0% -> 0%
where the time goes in v1:
time: 684 us; the launch traced here: 682 us
  waiting for transfers between devices  332 us (49%)
  blocking collectives  128 us (19%)
  other arithmetic  91.7 us (13%)
  local copies, waits for them, and re-layouts  62.2 us (9%)
  starting transfers between devices  27.4 us (4%)
  matrix products  25.1 us (4%)
  between operations  15.7 us (2%)
    all_to_all x1, waiting for transfers between devices, shards(): lax.all_to_all(outbound, 'dom', split_axis=0, concat_axis=0, tiled=True)  182 us
    psum x1, blocking collectives, shards(): grad_weight, grad_bias = lax.psum((weight_part, bias_part), 'dom')  128 us
    all_to_all x1, waiting for transfers between devices, receive_blocks(): lax.all_to_all(outgoing, 'dom', split_axis=0, concat_axis=0, tiled=True)  94.3 us
    psum x1, waiting for transfers between devices, shards(): grad_weight, grad_bias = lax.psum((weight_part, bias_part), 'dom')  44.9 us
    scatter-add x1, other arithmetic, shards(): per_slot = jax.ops.segment_sum(contrib, tile_sources, NB + peer_count * CAP)  33.1 us
    scatter-add x1, other arithmetic, shards(): aggregate = jax.ops.segment_sum(product, tile_rows, NB + 1)[:NB]  21.1 us
    scatter-add x1, other arithmetic, shards(): jax.ops.segment_sum(returned.reshape(peer_count * CAP, B, panel_width), t...  17 us
    all_to_all x1, starting transfers between devices, receive_blocks(): lax.all_to_all(outgoing, 'dom', split_axis=0, concat_axis=0, tiled=True)  14.8 us
  transfers between devices with their start and end apart: 5, of which 4 were waited for; matrix products, arithmetic and copies ran while one was open for 1% of the time, Pallas kernels for 0%

profile of v1, /device:TPU:1, one launch (start us, length us, event | category | flops | bytes accessed | tf_op | source)
XLA Modules:
  0.0 682.2 jit_solution(9730330559220744480)
XLA Ops:
  8.0 1.1 copy.18
  9.1 1.1 stack.2
  10.3 4.8 all-to-all-start
  16.0 0.7 iota_compare_fusion
  16.8 11.6 %all-to-all-done = bf16[4,1024,128]{1,2,0:T(8,128)(2,1)S(1)} async-done(((bf16[4,1024,128]{1,2,0:T(8,128)(2,1)}), bf16[4,1024,128]{1,2,0:T(8,128)(2,1)S(1)}, u32[]{:S(2)}, u32[]{:S(2)}) %all-to-all-start) | async-done | bytes 1048608 | tf_op jit(solution)/shard_map/all_to_all | solution.py:22
  28.8 3.1 gather_fusion
  31.9 4.5 broadcast_select_fusion.1
  36.4 14.8 %all-to-all-start.1 = ((bf16[64,2,128,128]{3,2,1,0:T(8,128)(2,1)}), bf16[64,2,128,128]{3,2,1,0:T(8,128)(2,1)}, u32[]{:S(2)}, u32[]{:S(2)}) async-start(bf16[64,2,128,128]{3,2,1,0:T(8,128)(2,1)} %broadcast_select_fusion.1), calls=%async_computation.1 | async-start | bytes 8388608 | tf_op jit(solution)/shard_map/all_to_all | solution.py:12
  51.3 94.3 %all-to-all-done.1 = bf16[64,2,128,128]{3,2,1,0:T(8,128)(2,1)} async-done(((bf16[64,2,128,128]{3,2,1,0:T(8,128)(2,1)}), bf16[64,2,128,128]{3,2,1,0:T(8,128)(2,1)}, u32[]{:S(2)}, u32[]{:S(2)}) %all-to-all-start.1) | async-done | bytes 4194336 | tf_op jit(solution)/shard_map/all_to_all | solution.py:12
  145.6 4.6 pad_maximum_fusion
  150.2 10.0 %gather_fusion.1 = bf16[160,128,128]{2,1,0:T(8,128)(2,1)} fusion(bf16[136,128,128]{2,1,0:T(8,128)(2,1)} %pad_maximum_fusion, s32[1024]{0:T(1024)S(1)} %pad_clamp_fusion.1), kind=kCustom, calls=%fused_computation.1 | custom fusion | bytes 10486400 | tf_op jit(solution)/shard_map/gather | solution.py:37
  160.2 11.8 %fusion.4 = f32[160,128,128]{1,2,0:T(8,128)} fusion(bf16[160,128,128]{2,1,0:T(8,128)(2,1)} %gather_fusion.1, bf16[1,160,128,128]{3,2,1,0:T(8,128)(2,1)} %param.13), kind=kOutput, calls=%fused_computation.13 | convolution fusion | flops 671088640 | bytes 20971520 | tf_op jit(solution)/shard_map/kab,kbf->kaf/dot_general | solution.py:36
  172.0 11.7 %copy.21 = f32[160,128,128]{2,1,0:T(8,128)} copy(f32[160,128,128]{1,2,0:T(8,128)} %fusion.4) | data formatting | bytes 20971520 | tf_op jit(solution)/shard_map/kab,kbf->kaf/dot_general | solution.py:36
  183.8 21.1 %scatter_fusion = f32[9,128,128]{2,1,0:T(8,128)S(1)} fusion(f32[9,128,128]{2,1,0:T(8,128)S(1)} %broadcast_in_dim.19, s32[160]{0:T(256)S(1)} %bitcast.63, f32[160,128,128]{2,1,0:T(8,128)} %copy.21), kind=kCustom, calls=%fused_computation.3 | custom fusion | flops 2621440 | bytes 31457920 | tf_op jit(solution)/shard_map/scatter-add | solution.py:39
  205.0 1.0 convert_reduce_fusion
  206.0 7.5 %gather_fusion.2 = bf16[160,128,128]{2,1,0:T(8,128)(2,1)} fusion(bf16[9,128,128]{2,1,0:T(8,128)(2,1)S(1)} %concatenate.7, s32[1024]{0:T(1024)S(1)} %pad_clamp_fusion), kind=kCustom, calls=%fused_computation.2 | custom fusion | bytes 10486400 | tf_op jit(solution)/shard_map/gather | solution.py:50
  213.5 9.8 %fusion.7 = f32[160,128,128]{1,2,0:T(8,128)} fusion(bf16[160,128,128]{2,1,0:T(8,128)(2,1)} %gather_fusion.2, bf16[1,160,128,128]{3,2,1,0:T(8,128)(2,1)} %param.13), kind=kOutput, calls=%fused_computation.14 | convolution fusion | flops 671088640 | bytes 20971520 | tf_op jit(solution)/shard_map/kab,kaf->kbf/dot_general | solution.py:49
  223.3 11.8 %copy.23 = f32[160,128,128]{2,1,0:T(8,128)} copy(f32[160,128,128]{1,2,0:T(8,128)} %fusion.7) | data formatting | bytes 20971520 | tf_op jit(solution)/shard_map/kab,kaf->kbf/dot_general | solution.py:49
  235.1 4.6 broadcast_in_dim.38
  239.7 33.1 %scatter_fusion.1 = f32[136,128,128]{2,1,0:T(8,128)} fusion(f32[136,128,128]{2,1,0:T(8,128)} %broadcast_in_dim.38, s32[160]{0:T(256)S(1)} %bitcast.64, f32[160,128,128]{2,1,0:T(8,128)} %copy.23), kind=kCustom, calls=%fused_computation.4 | custom fusion | flops 2621440 | bytes 31457920 | tf_op jit(solution)/shard_map/scatter-add | solution.py:52
  272.7 7.9 %slice.20 = f32[128,128,128]{2,1,0:T(8,128)} slice(f32[136,128,128]{2,1,0:T(8,128)} %scatter_fusion.1), slice={[8:136], [0:128], [0:128]} | slice | bytes 16777216 | tf_op jit(solution)/shard_map/slice | solution.py:53
  280.6 7.7 %all-to-all-start.2 = ((f32[64,2,128,128]{3,2,1,0:T(8,128)}), f32[64,2,128,128]{3,2,1,0:T(8,128)}, u32[]{:S(2)}, u32[]{:S(2)}) async-start(f32[64,2,128,128]{3,2,1,0:T(8,128)} %bitcast.55), calls=%async_computation.2 | async-start | bytes 16777216 | tf_op jit(solution)/shard_map/all_to_all | solution.py:54
  288.6 1.1 slice.19
  289.7 181.5 %all-to-all-done.2 = f32[64,2,128,128]{3,2,1,0:T(8,128)} async-done(((f32[64,2,128,128]{3,2,1,0:T(8,128)}), f32[64,2,128,128]{3,2,1,0:T(8,128)}, u32[]{:S(2)}, u32[]{:S(2)}) %all-to-all-start.2) | async-done | bytes 8388640 | tf_op jit(solution)/shard_map/all_to_all | solution.py:54
  471.2 7.2 %broadcast_select_fusion = f32[64,2,128,128]{3,2,1,0:T(8,128)} fusion(f32[64,2,128,128]{3,2,1,0:T(8,128)} %all-to-all-done.2, pred[64,2]{1,0:T(8,128)(4,1)S(1)} %iota_compare_fusion), kind=kLoop, calls=%fused_computation.11 | loop fusion | flops 2097152 | bytes 16777344 | tf_op jit(solution)/shard_map/jit(_where)/select_n | solution.py:56
  478.4 17.0 %scatter_fusion.2 = f32[8,128,128]{2,1,0:T(8,128)S(1)} fusion(f32[8,128,128]{2,1,0:T(8,128)S(1)} %slice.19, s32[128]{0:T(128)S(1)} %reshape.196, f32[128,128,128]{2,1,0:T(8,128)} %bitcast.56), kind=kCustom, calls=%fused_computation.5 | custom fusion | flops 2097152 | bytes 25166336 | tf_op jit(solution)/shard_map/scatter-add | solution.py:57
  495.5 1.2 convolution_bitcast_fusion
  496.7 1.8 fusion.10
  498.5 127.7 %psum.15 = f32[128]{0:T(128)} all-reduce(f32[128]{0:T(128)S(1)} %get-tuple-element.12), channel_id=1, replica_groups=mesh['dom'=64,'rep'=4] {'dom'}, use_global_device_ids=true, to_apply=%region_6.7 | all-reduce | flops 128 | bytes 1024 | tf_op jit(solution)/shard_map/psum | solution.py:63
  626.3 44.9 %all-reduce.3.cloned.1.call-done = f32[512,128]{0,1:T(8,128)} async-done(((f32[512,128]{0,1:T(8,128)}), f32[512,128]{0,1:T(8,128)}) %all-reduce.3.cloned.1.call-update) | async-done | bytes 262160 | tf_op jit(solution)/shard_map/psum | solution.py:63
  671.2 1.8 copy.25
  673.0 1.8 convert_element_type.35
  (33 shorter events, 2.0 us)
Async XLA Ops:
  8.0 20.3 %copy-start = (bf16[512,128]{1,0:T(8,128)(2,1)S(1)}, bf16[512,128]{1,0:T(8,128)(2,1)}, u32[]{:S(2)}) copy-start(bf16[512,128]{1,0:T(8,128)(2,1)} %param.10) | copy-start | bytes 393220
  10.3 18.1 %all-to-all-start = ((bf16[4,1024,128]{1,2,0:T(8,128)(2,1)}), bf16[4,1024,128]{1,2,0:T(8,128)(2,1)S(1)}, u32[]{:S(2)}, u32[]{:S(2)}) async-start(bf16[4,1024,128]{1,2,0:T(8,128)(2,1)} %stack.2), calls=%async_computation | async-start | bytes 2097152 | tf_op jit(solution)/shard_map/all_to_all | solution.py:22
  36.4 14.8 %copy-start.5 = (bf16[128]{0:T(256)(128)(2,1)S(1)}, bf16[128]{0:T(256)(128)(2,1)}, u32[]{:S(2)}) copy-start(bf16[128]{0:T(256)(128)(2,1)} %param.11) | copy-start | bytes 772
  36.4 14.8 %copy-start.3 = (s32[1,160]{1,0:T(1,128)S(1)}, s32[1,160]{1,0:T(1,128)}, u32[]{:S(2)}) copy-start(s32[1,160]{1,0:T(1,128)} %param.15) | copy-start | bytes 1924
  36.4 14.9 %copy-start.2 = (s32[1,160]{1,0:T(1,128)S(1)}, s32[1,160]{1,0:T(1,128)}, u32[]{:S(2)}) copy-start(s32[1,160]{1,0:T(1,128)} %param.14) | copy-start | bytes 1924
  36.4 109.2 %all-to-all-start.1 = ((bf16[64,2,128,128]{3,2,1,0:T(8,128)(2,1)}), bf16[64,2,128,128]{3,2,1,0:T(8,128)(2,1)}, u32[]{:S(2)}, u32[]{:S(2)}) async-start(bf16[64,2,128,128]{3,2,1,0:T(8,128)(2,1)} %broadcast_select_fusion.1), calls=%async_computation.1 | async-start | bytes 8388608 | tf_op jit(solution)/shard_map/all_to_all | solution.py:12
  183.8 21.2 %copy-start.1 = (bf16[1024,128]{1,0:T(8,128)(2,1)S(1)}, bf16[1024,128]{1,0:T(8,128)(2,1)}, u32[]{:S(2)}) copy-start(bf16[1024,128]{1,0:T(8,128)(2,1)} %param.12) | copy-start | bytes 786436
  280.6 7.7 %copy-start.4 = (s32[1,64,2]{1,2,0:T(2,128)S(1)}, s32[1,64,2]{1,2,0:T(2,128)}, u32[]{:S(2)}) copy-start(s32[1,64,2]{1,2,0:T(2,128)} %param.16) | copy-start | bytes 1540
  280.6 190.6 %all-to-all-start.2 = ((f32[64,2,128,128]{3,2,1,0:T(8,128)}), f32[64,2,128,128]{3,2,1,0:T(8,128)}, u32[]{:S(2)}, u32[]{:S(2)}) async-start(f32[64,2,128,128]{3,2,1,0:T(8,128)} %bitcast.55), calls=%async_computation.2 | async-start | bytes 16777216 | tf_op jit(solution)/shard_map/all_to_all | solution.py:54
  288.3 382.9 %all-reduce.3.cloned.1.call-start = ((), (), s32[]{:S(2)}) async-start(), calls=%async_computation.5 | async-start | bytes 524288 | tf_op jit(solution)/shard_map/psum | solution.py:63
  496.7 176.3 %reduce-scatter.2.cloned.1.call-start = ((), (), s32[]{:S(2)}) async-start(), calls=%async_computation.4 | async-start | bytes 2621440 | tf_op jit(solution)/shard_map/reduce_scatter | solution.py:65
Sparse Core Ops, SparseCore 0:
  496.8 174.3 all-reduce.2
Sparse Core Ops, SparseCore 1:
  499.7 30.5 reduce-scatter.1
